TPU v7x, 128 devices: a whole 4x4x4 slice. The times are simulated.
128 devices in a mesh: dp: 4 (over y), seq: 32 (over x, z, core).
Axes of the slice: x: 4, y: 4, z: 4, core: 2. Of those that a mesh axis runs over, the one named last changes fastest.
Arguments:
- tokens: bfloat16 [4, 16384, 1024], P('dp', 'seq'), may hold values from -18 to 18
- lengths: int32 [4, 128], P('dp'), may hold values from 1 to 128
- w_query: bfloat16 [1024, 512], replicated, may hold values from -0.1875 to 0.1875
- w_key: bfloat16 [1024, 512], replicated, may hold values from -0.1875 to 0.1875
- w_value: bfloat16 [1024, 512], replicated, may hold values from -0.1875 to 0.1875
- w_out: bfloat16 [512, 1024], replicated, may hold values from -2 to 2
- cotangent: bfloat16 [4, 16384, 1024], P('dp', 'seq'), may hold values from -6 to 6
Outputs:
- mixed: bfloat16 [4, 16384, 1024], P('dp', 'seq')
- grad_tokens: bfloat16 [4, 16384, 1024], P('dp', 'seq')
- grad_query: float32 [1024, 512], replicated
- grad_key: float32 [1024, 512], replicated
- grad_value: float32 [1024, 512], replicated
- grad_output: float32 [512, 1024], replicated
All inputs are finite; a program needn't handle non-finite values.
Results may differ from a plain program's by a relative error of at most 0.014.
The roundings to bfloat16 on the way count: a program that leaves them out, or rounds other values in their place, can miss the bound.
Values may be sent and summed in bfloat16 or wider, within the bound.
A program may use at most 192 MiB of HBM per device.

v0:
```python
import math
import jax
import jax.numpy as jnp
from jax import lax
from jax.sharding import PartitionSpec as P

HEADS = 4
TILE = 128
bar_offsets = (0, 1, 2, 4, 8, 12, 16, 24, 32)
group_bars = 4
far_score = -1e30


def sent_to_all(shard, axis):
    count = lax.axis_size(axis)
    return lax.all_to_all(
        jnp.broadcast_to(shard[None], (count, *shard.shape)), axis, 0, 0, tiled=True
    )


def joined_along(parts, dim):
    parts = jnp.moveaxis(parts, 0, dim)
    shape = parts.shape
    return parts.reshape(*shape[:dim], shape[dim] * shape[dim + 1], *shape[dim + 2 :])


def collect(shard, axis, dim):
    parts = sent_to_all(shard, axis)
    return joined_along(parts, dim)


def side_by_side(arrays, axis, dim, along):
    both = jnp.concatenate(arrays, axis=along)
    whole, at, gathered = (collect(both, axis, dim), 0, [])
    for a in arrays:
        gathered.append(lax.slice_in_dim(whole, at, at + a.shape[along], axis=along))
        at += a.shape[along]
    return tuple(gathered)


def shifted(block, axis, distance):
    devices = range(lax.axis_size(axis))
    route = [(i - distance, i) for i in devices if i - distance in devices]
    return lax.ppermute(block, axis, route)


def split_up(shard, dim, count):
    shape = shard.shape
    parts = shard.reshape(*shape[:dim], count, shape[dim] // count, *shape[dim + 1 :])
    return jnp.moveaxis(parts, dim, 0)


def sent_and_summed(shard, axis, dim):
    parts = split_up(shard, dim, lax.axis_size(axis))
    arrived = lax.all_to_all(parts, axis, split_axis=0, concat_axis=0, tiled=True)
    return arrived.astype(jnp.float32).sum(axis=0)


def in_one_piece(arrays, axis, dim, along):
    ends, at = ([], 0)
    for a in arrays[:-1]:
        at += a.shape[along]
        ends.append(at)
    both = jnp.concatenate(arrays, axis=along)
    return tuple(jnp.split(sent_and_summed(both, axis, dim), ends, axis=along))


def product(form, left, right):
    return jnp.einsum(form, left, right, preferred_element_type=jnp.float32)


def summarize(bar_rows, length):
    slot_ids = jnp.arange(bar_rows.shape[1], dtype=jnp.int32)
    live_slots = slot_ids[None, :] < length[:, None]
    running = jnp.sum(jnp.where(live_slots[:, :, None], bar_rows.astype(jnp.float32), 0.0), axis=1)
    return (running / length[:, None].astype(jnp.float32)).astype(jnp.bfloat16)


def bar_block(
    queries,
    ext_key,
    ext_value,
    ext_length,
    base_bar,
    bar_ids,
    query_length,
    summary_key,
    summary_value,
    grad_context,
):
    group_count, tile_len, head_count, head_dim = queries.shape
    sources = len(bar_offsets)
    key_parts = []
    value_parts = []
    length_parts = []
    for offset in bar_offsets:
        first_bar = base_bar - offset
        key_parts.append(lax.dynamic_slice_in_dim(ext_key, first_bar, group_count, 0))
        value_parts.append(lax.dynamic_slice_in_dim(ext_value, first_bar, group_count, 0))
        length_parts.append(lax.dynamic_slice_in_dim(ext_length, first_bar, group_count, 0))
    fine_key = jnp.stack(key_parts, 1).reshape(
        group_count, sources * tile_len, head_count, head_dim
    )
    fine_value = jnp.stack(value_parts, 1).reshape(
        group_count, sources * tile_len, head_count, head_dim
    )
    fine_length = jnp.stack(length_parts, 1)
    slot_ids = jnp.arange(tile_len, dtype=jnp.int32)
    key_live = slot_ids[None, None, :] < fine_length[:, :, None]
    causal = slot_ids[None, :] <= slot_ids[:, None]
    other_bar = jnp.arange(sources, dtype=jnp.int32) != 0
    fine_live = key_live[:, None, :, :] & (
        causal[None, :, None, :] | other_bar[None, None, :, None]
    )
    fine_live = fine_live.reshape(group_count, 1, tile_len, sources * tile_len)
    distance = bar_ids[:, None] - jnp.arange(summary_key.shape[0], dtype=jnp.int32)[None, :]
    coarse_live = distance >= 1
    for offset in bar_offsets[1:]:
        coarse_live = coarse_live & (distance != offset)
    coarse_live = coarse_live[:, None, None, :]
    score_scale = 1.0 / math.sqrt(head_dim)
    fine_score = product("gqhe,gkhe->ghqk", queries, fine_key) * score_scale
    coarse_score = product("gqhe,nhe->ghqn", queries, summary_key) * score_scale
    fine_score = jnp.where(fine_live, fine_score, far_score)
    coarse_score = jnp.where(coarse_live, coarse_score, far_score)
    top_score = jnp.maximum(jnp.max(fine_score, axis=-1), jnp.max(coarse_score, axis=-1))[..., None]
    fine_exp = jnp.where(fine_live, jnp.exp(fine_score - top_score), 0.0)
    coarse_exp = jnp.where(coarse_live, jnp.exp(coarse_score - top_score), 0.0)
    denominator = (jnp.sum(fine_exp, axis=-1) + jnp.sum(coarse_exp, axis=-1))[..., None]
    fine_prob = fine_exp / denominator
    coarse_prob = coarse_exp / denominator
    fine_round = fine_prob.astype(jnp.bfloat16)
    coarse_round = coarse_prob.astype(jnp.bfloat16)
    attended_context = product("ghqk,gkhe->gqhe", fine_round, fine_value) + product(
        "ghqn,nhe->gqhe", coarse_round, summary_value
    )
    query_live = slot_ids[None, :] < query_length[:, None]
    attended_context = jnp.where(query_live[:, :, None, None], attended_context, 0.0)
    fine_dp = product("gqhe,gkhe->ghqk", grad_context, fine_value)
    coarse_dp = product("gqhe,nhe->ghqn", grad_context, summary_value)
    delta = (jnp.sum(fine_prob * fine_dp, axis=-1) + jnp.sum(coarse_prob * coarse_dp, axis=-1))[
        ..., None
    ]
    fine_ds = (fine_prob * (fine_dp - delta) * score_scale).astype(jnp.bfloat16)
    coarse_ds = (coarse_prob * (coarse_dp - delta) * score_scale).astype(jnp.bfloat16)
    query_gradient_rows = product("ghqk,gkhe->gqhe", fine_ds, fine_key) + product(
        "ghqn,nhe->gqhe", coarse_ds, summary_key
    )
    fine_gk = product("ghqk,gqhe->gkhe", fine_ds, queries).reshape(
        group_count, sources, tile_len, head_count, head_dim
    )
    fine_gv = product("ghqk,gqhe->gkhe", fine_round, grad_context).reshape(
        group_count, sources, tile_len, head_count, head_dim
    )
    coarse_key_gradient = product("ghqn,gqhe->nhe", coarse_ds, queries)
    coarse_value_gradient = product("ghqn,gqhe->nhe", coarse_round, grad_context)
    return (
        attended_context,
        query_gradient_rows,
        fine_gk,
        fine_gv,
        coarse_key_gradient,
        coarse_value_gradient,
    )


def spread(running, grads, base_bar):
    group_count = grads.shape[0]
    for position, offset in enumerate(bar_offsets):
        first_bar = base_bar - offset
        current = lax.dynamic_slice_in_dim(running, first_bar, group_count, 0)
        running = lax.dynamic_update_slice_in_dim(
            running, current + grads[:, position], first_bar, 0
        )
    return running


def local(tokens, lengths, w_query, w_key, w_value, w_out, cotangent):
    inputs = tokens[0]
    grad_out = cotangent[0]
    token_count = inputs.shape[0]
    inner_width = w_query.shape[1]
    head_dim = inner_width // HEADS
    bar_count = token_count // TILE
    reach_dev = max(bar_offsets[-1] // bar_count, 1)
    queries = jnp.dot(inputs, w_query, preferred_element_type=jnp.float32).astype(jnp.bfloat16)
    keys_own = jnp.dot(inputs, w_key, preferred_element_type=jnp.float32).astype(jnp.bfloat16)
    values_own = jnp.dot(inputs, w_value, preferred_element_type=jnp.float32).astype(jnp.bfloat16)
    all_length = lengths[0]
    first_own = lax.axis_index("seq") * bar_count
    local_length = lax.dynamic_slice_in_dim(all_length, first_own, bar_count, 0)
    slot_ids = jnp.arange(TILE, dtype=jnp.int32)
    live_slots = slot_ids[None, :] < local_length[:, None]
    token_live = live_slots.reshape(-1)
    own_summary = (
        summarize(keys_own.reshape(bar_count, TILE, inner_width), local_length),
        summarize(values_own.reshape(bar_count, TILE, inner_width), local_length),
    )
    summary_key, summary_value = side_by_side((own_summary[0], own_summary[1]), "seq", 0, 1)
    summary_key = summary_key.reshape(-1, HEADS, head_dim)
    summary_value = summary_value.reshape(-1, HEADS, head_dim)
    grad_context = jnp.dot(grad_out, w_out.T, preferred_element_type=jnp.float32)
    grad_context = jnp.where(token_live[:, None], grad_context, 0.0).astype(jnp.bfloat16)
    key_list = [keys_own]
    value_list = [values_own]
    for distance in range(1, reach_dev + 1):
        arrived = shifted((keys_own, values_own), "seq", distance)
        key_list.append(arrived[0])
        value_list.append(arrived[1])
    key_stack = jnp.stack(key_list, 0)
    value_stack = jnp.stack(value_list, 0)
    ext_bars = (reach_dev + 1) * bar_count
    ext_key = key_stack[::-1].reshape(ext_bars, TILE, HEADS, head_dim)
    ext_value = value_stack[::-1].reshape(ext_bars, TILE, HEADS, head_dim)
    padded_length = jnp.concatenate([jnp.zeros((reach_dev * bar_count,), jnp.int32), all_length], 0)
    ext_length = lax.dynamic_slice_in_dim(padded_length, first_own, ext_bars, 0)
    query_bars = queries.reshape(bar_count, TILE, HEADS, head_dim)
    grad_bars = grad_context.reshape(bar_count, TILE, HEADS, head_dim)

    def step(carried_state, block_index):
        accumulated_key, accumulated_value, accumulated_summary_key, accumulated_summary_value = (
            carried_state
        )
        begin_bar = block_index * group_bars
        base_bar = reach_dev * bar_count + begin_bar
        bar_ids = first_own + begin_bar + jnp.arange(group_bars, dtype=jnp.int32)
        result = bar_block(
            query_bars,
            ext_key,
            ext_value,
            ext_length,
            base_bar,
            bar_ids,
            local_length,
            summary_key,
            summary_value,
            grad_bars,
        )
        (
            attended_context,
            query_gradient_rows,
            fine_gk,
            fine_gv,
            coarse_key_gradient,
            coarse_value_gradient,
        ) = result
        accumulated_key = spread(accumulated_key, fine_gk, base_bar)
        accumulated_value = spread(accumulated_value, fine_gv, base_bar)
        return (
            (
                accumulated_key,
                accumulated_value,
                accumulated_summary_key + coarse_key_gradient,
                accumulated_summary_value + coarse_value_gradient,
            ),
            (attended_context.astype(jnp.bfloat16), query_gradient_rows.astype(jnp.bfloat16)),
        )

    ext_zero = jnp.zeros((ext_bars, TILE, HEADS, head_dim), jnp.float32)
    sum_zero = jnp.zeros(summary_key.shape, jnp.float32)
    carried_state, stacked = lax.scan(
        step,
        (ext_zero, ext_zero, sum_zero, sum_zero),
        jnp.arange(bar_count // group_bars, dtype=jnp.int32),
    )
    accumulated_key, accumulated_value, accumulated_summary_key, accumulated_summary_value = (
        carried_state
    )
    attended_context = stacked[0].reshape(token_count, inner_width)
    query_gradient_rows = stacked[1].reshape(token_count, inner_width)
    grad_key_stack = accumulated_key.reshape(reach_dev + 1, token_count, inner_width)[::-1]
    grad_value_stack = accumulated_value.reshape(reach_dev + 1, token_count, inner_width)[::-1]
    own_key = grad_key_stack[0]
    own_value = grad_value_stack[0]
    for distance in range(1, reach_dev + 1):
        returned = (
            shifted(grad_key_stack[distance].astype(jnp.bfloat16), "seq", -distance).astype(
                jnp.float32
            ),
            shifted(grad_value_stack[distance].astype(jnp.bfloat16), "seq", -distance).astype(
                jnp.float32
            ),
        )
        own_key = own_key + returned[0]
        own_value = own_value + returned[1]
    summary_back = in_one_piece(
        (
            accumulated_summary_key.astype(jnp.bfloat16),
            accumulated_summary_value.astype(jnp.bfloat16),
        ),
        "seq",
        0,
        1,
    )
    inverse_denominator = 1.0 / local_length.astype(jnp.float32)
    shared_key_rows = summary_back[0].reshape(bar_count, inner_width) * inverse_denominator[:, None]
    share_value = summary_back[1].reshape(bar_count, inner_width) * inverse_denominator[:, None]
    own_key = own_key.reshape(bar_count, TILE, inner_width) + jnp.where(
        live_slots[:, :, None], shared_key_rows[:, None, :], 0.0
    )
    own_value = own_value.reshape(bar_count, TILE, inner_width) + jnp.where(
        live_slots[:, :, None], share_value[:, None, :], 0.0
    )
    grad_keys = own_key.reshape(token_count, inner_width).astype(jnp.bfloat16)
    grad_values = own_value.reshape(token_count, inner_width).astype(jnp.bfloat16)
    mixed = jnp.dot(attended_context, w_out, preferred_element_type=jnp.float32).astype(
        jnp.bfloat16
    )
    grad_in = (
        product("te,de->td", query_gradient_rows, w_query)
        + product("te,de->td", grad_keys, w_key)
        + product("te,de->td", grad_values, w_value)
    )
    weight_terms = (
        product("td,te->de", inputs, query_gradient_rows),
        product("td,te->de", inputs, grad_keys),
        product("td,te->de", inputs, grad_values),
        product("te,td->ed", attended_context, grad_out),
    )
    summed = (
        lax.psum(weight_terms[0].astype(jnp.bfloat16), ("dp", "seq")).astype(jnp.float32),
        lax.psum(weight_terms[1].astype(jnp.bfloat16), ("dp", "seq")).astype(jnp.float32),
        lax.psum(weight_terms[2].astype(jnp.bfloat16), ("dp", "seq")).astype(jnp.float32),
        lax.psum(weight_terms[3].astype(jnp.bfloat16), ("dp", "seq")).astype(jnp.float32),
    )
    return (
        mixed[None],
        grad_in.astype(jnp.bfloat16)[None],
        summed[0],
        summed[1],
        summed[2],
        summed[3],
    )


def solution(mesh):
    placed = (P("dp", "seq", None), P("dp", None), P(), P(), P(), P(), P("dp", "seq", None))
    return jax.shard_map(
        local,
        mesh=mesh,
        in_specs=placed,
        out_specs=(P("dp", "seq", None), P("dp", "seq", None), P(), P(), P(), P()),
        check_vma=False,
    )
```

profile of v0, /device:TPU:1, one launch (start us, length us, event | category | flops | bytes accessed | tf_op | source)
XLA Modules:
  0.0 742.3 jit_solution(1753987246523534247)
XLA Ops:
  11.3 4.9 collective-permute-start.15
  20.2 5.3 collective-permute-start.10
  37.1 4.8 all-to-all-start
  56.2 21.3 %all-to-all-done = bf16[32,4,1024]{2,1,0:T(4,128)(2,1)S(1)} async-done(((bf16[32,4,1024]{2,1,0:T(4,128)(2,1)}), bf16[32,4,1024]{2,1,0:T(4,128)(2,1)S(1)}, u32[]{:S(2)}, u32[]{:S(2)}) %all-to-all-start) | async-done | bytes 262176 | tf_op jit(solution)/shard_map/all_to_all | solution.py:16
  95.5 4.8 collective-permute-start.7
  101.1 11.5 %collective-permute-done.12 = bf16[512,512]{1,0:T(8,128)(2,1)S(1)} collective-permute-done((bf16[512,512]{1,0:T(8,128)(2,1)}, bf16[512,512]{1,0:T(8,128)(2,1)S(1)}, u32[]{:S(2)}, u32[]{:S(2)}) %collective-permute-start.12) | collective-permute-done | bytes 524320 | tf_op jit(solution)/shard_map/ppermute | solution.py:44
  118.3 6.4 collective-permute-start.4
  125.5 5.2 collective-permute-start.1
  141.1 7.7 %reshape.379 = bf16[36,128,4,128]{3,2,1,0:T(4,128)(2,1)} reshape(bf16[9,512,512]{2,1,0:T(8,128)(2,1)} %rev.9) | data formatting | bytes 9437184 | tf_op jit(solution)/shard_map/reshape | solution.py:213
  159.1 25.7 %collective-permute-start.3 = (bf16[512,512]{1,0:T(8,128)(2,1)}, bf16[512,512]{1,0:T(8,128)(2,1)}, u32[]{:S(2)}, u32[]{:S(2)}) collective-permute-start(bf16[512,512]{1,0:T(8,128)(2,1)} %get-tuple-element.136), channel_id=1, source_target_pairs={{0,4},{1,5},{2,6},{3,7},{4,8},{5,9},{6,10},{7,11},{8,12},{9,13},{1... | collective-permute-start | bytes 1572872 | tf_op jit(solution)/shard_map/ppermute | solution.py:44
  216.6 5.7 copy.316
  227.9 4.9 rev.8
  232.7 7.7 %reshape.376 = bf16[36,128,4,128]{3,2,1,0:T(4,128)(2,1)} reshape(bf16[9,512,512]{2,1,0:T(8,128)(2,1)} %rev.8) | data formatting | bytes 9437184 | tf_op jit(solution)/shard_map/reshape | solution.py:214
  276.0 10.1 %fusion.16 = f32[4,128,4,128]{1,3,2,0:T(8,128)} fusion(bf16[4,1152,4,128]{3,1,2,0:T(8,128)(2,1)} %bitcast.13, f32[4,4,128,1152]{3,2,1,0:T(8,128)} %copy-done.1, f32[4,4,128]{2,1,0:T(4,128)S(1)} %copy_add_fusion.1, f32[4,4,128]{2,1,0:T(4,128)S(1)} %copy_maximum_fusion, pred[4,128,1152]{2,1,0:T(8,128)(4,1)S(1)} %broadcast_and_fusion), kind=kOutput, calls=%fused_computation.36 | convolution fusion | flops 618135552 | bytes 15810560 | tf_op jit(solution)/shard_map/while/body/eval_jaxpr/ghqk,gkhe->gqhe/dot_general | solution.py:69
  286.1 6.9 multiply_reduce_fusion
  293.1 5.9 convolution_bitcast_fusion
  306.5 4.9 convolution_bitcast_fusion.1
  311.4 9.6 %copy.338 = f32[4,1152,4,128]{3,1,2,0:T(8,128)} copy(f32[4,1152,4,128]{1,3,2,0:T(8,128)} %convolution_bitcast_fusion.1) | data formatting | bytes 18874368 | tf_op jit(solution)/shard_map/while/body/eval_jaxpr/ghqk,gqhe->gkhe/transpose | solution.py:69
  338.4 10.1 %copy.362 = f32[4,1152,4,128]{3,1,2,0:T(8,128)} copy(f32[4,1152,4,128]{1,3,2,0:T(8,128)} %convolution_bitcast_fusion) | data formatting | bytes 18874368 | tf_op jit(solution)/shard_map/while/body/eval_jaxpr/ghqk,gqhe->gkhe/transpose | solution.py:69
  354.4 14.8 %all-to-all-start.1 = ((bf16[32,4,8,128]{3,1,2,0:T(4,128)(2,1)}), bf16[32,4,8,128]{3,1,2,0:T(4,128)(2,1)S(1)}, u32[]{:S(2)}, u32[]{:S(2)}) async-start(bf16[32,4,8,128]{3,1,2,0:T(4,128)(2,1)} %copy.358), calls=%async_computation.1 | async-start | bytes 524288 | tf_op jit(solution)/shard_map/all_to_all | solution.py:55
  416.7 11.3 %collective-permute-done.22 = bf16[512,512]{1,0:T(8,128)(2,1)} collective-permute-done((bf16[512,512]{1,0:T(8,128)(2,1)}, bf16[512,512]{1,0:T(8,128)(2,1)}, u32[]{:S(2)}, u32[]{:S(2)}) %collective-permute-start.22) | collective-permute-done | bytes 524320 | tf_op jit(solution)/shard_map/ppermute | solution.py:44
  431.3 18.0 %collective-permute-done.23 = bf16[512,512]{1,0:T(8,128)(2,1)} collective-permute-done((bf16[512,512]{1,0:T(8,128)(2,1)}, bf16[512,512]{1,0:T(8,128)(2,1)}, u32[]{:S(2)}, u32[]{:S(2)}) %collective-permute-start.23) | collective-permute-done | bytes 524320 | tf_op jit(solution)/shard_map/ppermute | solution.py:44
  474.5 48.7 %collective-permute-done.30 = bf16[512,512]{1,0:T(8,128)(2,1)} collective-permute-done((bf16[512,512]{1,0:T(8,128)(2,1)}, bf16[512,512]{1,0:T(8,128)(2,1)}, u32[]{:S(2)}, u32[]{:S(2)}) %collective-permute-start.30) | collective-permute-done | bytes 524320 | tf_op jit(solution)/shard_map/ppermute | solution.py:44
  548.1 178.6 %all-reduce.6.cloned.1.call-done = (bf16[1024,512]{0,1:T(8,128)(2,1)}, bf16[1024,512]{0,1:T(8,128)(2,1)}, bf16[1024,512]{0,1:T(8,128)(2,1)}, bf16[512,1024]{1,0:T(8,128)(2,1)}) async-done(((bf16[1024,512]{0,1:T(8,128)(2,1)}, bf16[1024,512]{0,1:T(8,128)(2,1)}, bf16[1024,512]{0,1:T(8,128)(2,1)}, bf16[512,1024]{1,0:T(8,128)(2,1)}), (bf16[1024,512]{0,1:T(8,128)(2,1)}, bf16[1024,512]{0,1:T(8,128)(2,1)}, ...) | async-done | bytes 4194320 | tf_op jit(solution)/shard_map/psum | solution.py:321
  (338 shorter events, 292.2 us)
Async XLA Ops:
  11.3 121.3 %collective-permute-start.15 = (bf16[512,512]{1,0:T(8,128)(2,1)}, bf16[512,512]{1,0:T(8,128)(2,1)}, u32[]{:S(2)}, u32[]{:S(2)}) collective-permute-start(bf16[512,512]{1,0:T(8,128)(2,1)} %get-tuple-element.138), channel_id=1, source_target_pairs={{0,8},{1,9},{2,10},{3,11},{4,12},{5,13},{6,14},{7,15},{8,16},{9,17... | collective-permute-start | bytes 1572872 | tf_op jit(solution)/shard_map/ppermute | solution.py:44
  16.2 109.3 %collective-permute-start.14 = (bf16[512,512]{1,0:T(8,128)(2,1)}, bf16[512,512]{1,0:T(8,128)(2,1)}, u32[]{:S(2)}, u32[]{:S(2)}) collective-permute-start(bf16[512,512]{1,0:T(8,128)(2,1)} %get-tuple-element.138), channel_id=1, source_target_pairs={{0,7},{1,8},{2,9},{3,10},{4,11},{5,12},{6,13},{7,14},{8,15},{9,16}... | collective-permute-start | bytes 1572872 | tf_op jit(solution)/shard_map/ppermute | solution.py:44
  20.2 71.2 %collective-permute-start.10 = (bf16[512,512]{1,0:T(8,128)(2,1)}, bf16[512,512]{1,0:T(8,128)(2,1)}, u32[]{:S(2)}, u32[]{:S(2)}) collective-permute-start(bf16[512,512]{1,0:T(8,128)(2,1)} %get-tuple-element.138), channel_id=1, source_target_pairs={{0,3},{1,4},{2,5},{3,6},{4,7},{5,8},{6,9},{7,10},{8,11},{9,12},{10... | collective-permute-start | bytes 1572872 | tf_op jit(solution)/shard_map/ppermute | solution.py:44
  25.5 59.8 %collective-permute-start.9 = (bf16[512,512]{1,0:T(8,128)(2,1)}, bf16[512,512]{1,0:T(8,128)(2,1)}, u32[]{:S(2)}, u32[]{:S(2)}) collective-permute-start(bf16[512,512]{1,0:T(8,128)(2,1)} %get-tuple-element.138), channel_id=1, source_target_pairs={{0,2},{1,3},{2,4},{3,5},{4,6},{5,7},{6,8},{7,9},{8,10},{9,11},{10,... | collective-permute-start | bytes 1572872 | tf_op jit(solution)/shard_map/ppermute | solution.py:44
  28.4 52.4 %collective-permute-start.8 = (bf16[512,512]{1,0:T(8,128)(2,1)}, bf16[512,512]{1,0:T(8,128)(2,1)}, u32[]{:S(2)}, u32[]{:S(2)}) collective-permute-start(bf16[512,512]{1,0:T(8,128)(2,1)} %get-tuple-element.138), channel_id=1, source_target_pairs={{0,1},{1,2},{2,3},{3,4},{4,5},{5,6},{6,7},{7,8},{8,9},{9,10},{10,1... | collective-permute-start | bytes 1572872 | tf_op jit(solution)/shard_map/ppermute | solution.py:44
  37.1 40.4 %all-to-all-start = ((bf16[32,4,1024]{2,1,0:T(4,128)(2,1)}), bf16[32,4,1024]{2,1,0:T(4,128)(2,1)S(1)}, u32[]{:S(2)}, u32[]{:S(2)}) async-start(bf16[32,4,1024]{2,1,0:T(4,128)(2,1)} %broadcast_in_dim.191), calls=%async_computation | async-start | bytes 524288 | tf_op jit(solution)/shard_map/all_to_all | solution.py:16
  95.5 130.5 %collective-permute-start.7 = (bf16[512,512]{1,0:T(8,128)(2,1)}, bf16[512,512]{1,0:T(8,128)(2,1)}, u32[]{:S(2)}, u32[]{:S(2)}) collective-permute-start(bf16[512,512]{1,0:T(8,128)(2,1)} %get-tuple-element.136), channel_id=1, source_target_pairs={{0,8},{1,9},{2,10},{3,11},{4,12},{5,13},{6,14},{7,15},{8,16},{9,17... | collective-permute-start | bytes 1572872 | tf_op jit(solution)/shard_map/ppermute | solution.py:44
  112.6 111.5 %collective-permute-start.6 = (bf16[512,512]{1,0:T(8,128)(2,1)}, bf16[512,512]{1,0:T(8,128)(2,1)}, u32[]{:S(2)}, u32[]{:S(2)}) collective-permute-start(bf16[512,512]{1,0:T(8,128)(2,1)} %get-tuple-element.136), channel_id=1, source_target_pairs={{0,7},{1,8},{2,9},{3,10},{4,11},{5,12},{6,13},{7,14},{8,15},{9,16}... | collective-permute-start | bytes 1572872 | tf_op jit(solution)/shard_map/ppermute | solution.py:44
  118.3 78.3 %collective-permute-start.4 = (bf16[512,512]{1,0:T(8,128)(2,1)}, bf16[512,512]{1,0:T(8,128)(2,1)}, u32[]{:S(2)}, u32[]{:S(2)}) collective-permute-start(bf16[512,512]{1,0:T(8,128)(2,1)} %get-tuple-element.136), channel_id=1, source_target_pairs={{0,5},{1,6},{2,7},{3,8},{4,9},{5,10},{6,11},{7,12},{8,13},{9,14},{... | collective-permute-start | bytes 1572872 | tf_op jit(solution)/shard_map/ppermute | solution.py:44
  154.8 35.8 %collective-permute-start.2 = (bf16[512,512]{1,0:T(8,128)(2,1)}, bf16[512,512]{1,0:T(8,128)(2,1)}, u32[]{:S(2)}, u32[]{:S(2)}) collective-permute-start(bf16[512,512]{1,0:T(8,128)(2,1)} %get-tuple-element.136), channel_id=1, source_target_pairs={{0,3},{1,4},{2,5},{3,6},{4,7},{5,8},{6,9},{7,10},{8,11},{9,12},{10... | collective-permute-start | bytes 1572872 | tf_op jit(solution)/shard_map/ppermute | solution.py:44
  354.4 113.5 %all-to-all-start.1 = ((bf16[32,4,8,128]{3,1,2,0:T(4,128)(2,1)}), bf16[32,4,8,128]{3,1,2,0:T(4,128)(2,1)S(1)}, u32[]{:S(2)}, u32[]{:S(2)}) async-start(bf16[32,4,8,128]{3,1,2,0:T(4,128)(2,1)} %copy.358), calls=%async_computation.1 | async-start | bytes 524288 | tf_op jit(solution)/shard_map/all_to_all | solution.py:55
  369.2 357.5 %all-reduce.6.cloned.1.call-start = ((), (), s32[]{:S(2)}) async-start(), calls=%async_computation.2 | async-start | bytes 8388608 | tf_op jit(solution)/shard_map/psum | solution.py:321
  384.5 43.6 %collective-permute-start.22 = (bf16[512,512]{1,0:T(8,128)(2,1)}, bf16[512,512]{1,0:T(8,128)(2,1)}, u32[]{:S(2)}, u32[]{:S(2)}) collective-permute-start(bf16[512,512]{1,0:T(8,128)(2,1)} %bitcast.488), channel_id=1, source_target_pairs={{7,0},{8,1},{9,2},{10,3},{11,4},{12,5},{13,6},{14,7},{15,8},{16,9}... | collective-permute-start | bytes 1572872 | tf_op jit(solution)/shard_map/ppermute | solution.py:44
  385.8 44.2 %collective-permute-start.21 = (bf16[512,512]{1,0:T(8,128)(2,1)}, bf16[512,512]{1,0:T(8,128)(2,1)}, u32[]{:S(2)}, u32[]{:S(2)}) collective-permute-start(bf16[512,512]{1,0:T(8,128)(2,1)} %bitcast.489), channel_id=1, source_target_pairs={{6,0},{7,1},{8,2},{9,3},{10,4},{11,5},{12,6},{13,7},{14,8},{15,9},... | collective-permute-start | bytes 1572872 | tf_op jit(solution)/shard_map/ppermute | solution.py:44
  387.1 62.1 %collective-permute-start.23 = (bf16[512,512]{1,0:T(8,128)(2,1)}, bf16[512,512]{1,0:T(8,128)(2,1)}, u32[]{:S(2)}, u32[]{:S(2)}) collective-permute-start(bf16[512,512]{1,0:T(8,128)(2,1)} %bitcast.487), channel_id=1, source_target_pairs={{8,0},{9,1},{10,2},{11,3},{12,4},{13,5},{14,6},{15,7},{16,8},{17,9... | collective-permute-start | bytes 1572872 | tf_op jit(solution)/shard_map/ppermute | solution.py:44
  409.9 40.6 %collective-permute-start.18 = (bf16[512,512]{1,0:T(8,128)(2,1)S(1)}, bf16[512,512]{1,0:T(8,128)(2,1)}, u32[]{:S(2)}, u32[]{:S(2)}) collective-permute-start(bf16[512,512]{1,0:T(8,128)(2,1)S(1)} %bitcast.542), channel_id=1, source_target_pairs={{3,0},{4,1},{5,2},{6,3},{7,4},{8,5},{9,6},{10,7},{11,8},{12,9},{13... | collective-permute-start | bytes 1572872 | tf_op jit(solution)/shard_map/ppermute | solution.py:44
  415.4 52.5 %collective-permute-start.19 = (bf16[512,512]{1,0:T(8,128)(2,1)}, bf16[512,512]{1,0:T(8,128)(2,1)}, u32[]{:S(2)}, u32[]{:S(2)}) collective-permute-start(bf16[512,512]{1,0:T(8,128)(2,1)} %bitcast.491), channel_id=1, source_target_pairs={{4,0},{5,1},{6,2},{7,3},{8,4},{9,5},{10,6},{11,7},{12,8},{13,9},{1... | collective-permute-start | bytes 1572872 | tf_op jit(solution)/shard_map/ppermute | solution.py:44
  428.0 41.2 %collective-permute-start.16 = (bf16[512,512]{1,0:T(8,128)(2,1)}, bf16[512,512]{1,0:T(8,128)(2,1)}, u32[]{:S(2)}, u32[]{:S(2)}) collective-permute-start(bf16[512,512]{1,0:T(8,128)(2,1)} %bitcast.494), channel_id=1, source_target_pairs={{1,0},{2,1},{3,2},{4,3},{5,4},{6,5},{7,6},{8,7},{9,8},{10,9},{11,1... | collective-permute-start | bytes 1572872 | tf_op jit(solution)/shard_map/ppermute | solution.py:44
  430.0 42.0 %collective-permute-start.25 = (bf16[512,512]{1,0:T(8,128)(2,1)}, bf16[512,512]{1,0:T(8,128)(2,1)}, u32[]{:S(2)}, u32[]{:S(2)}) collective-permute-start(bf16[512,512]{1,0:T(8,128)(2,1)} %bitcast.485), channel_id=1, source_target_pairs={{2,0},{3,1},{4,2},{5,3},{6,4},{7,5},{8,6},{9,7},{10,8},{11,9},{12,... | collective-permute-start | bytes 1572872 | tf_op jit(solution)/shard_map/ppermute | solution.py:44
  450.5 72.7 %collective-permute-start.30 = (bf16[512,512]{1,0:T(8,128)(2,1)}, bf16[512,512]{1,0:T(8,128)(2,1)}, u32[]{:S(2)}, u32[]{:S(2)}) collective-permute-start(bf16[512,512]{1,0:T(8,128)(2,1)} %bitcast.480), channel_id=1, source_target_pairs={{7,0},{8,1},{9,2},{10,3},{11,4},{12,5},{13,6},{14,7},{15,8},{16,9}... | collective-permute-start | bytes 1572872 | tf_op jit(solution)/shard_map/ppermute | solution.py:44
  468.0 62.1 %collective-permute-start.29 = (bf16[512,512]{1,0:T(8,128)(2,1)}, bf16[512,512]{1,0:T(8,128)(2,1)S(1)}, u32[]{:S(2)}, u32[]{:S(2)}) collective-permute-start(bf16[512,512]{1,0:T(8,128)(2,1)} %bitcast.547), channel_id=1, source_target_pairs={{6,0},{7,1},{8,2},{9,3},{10,4},{11,5},{12,6},{13,7},{14,8},{15,9},... | collective-permute-start | bytes 1572872 | tf_op jit(solution)/shard_map/ppermute | solution.py:44
  469.3 63.5 %collective-permute-start.31 = (bf16[512,512]{1,0:T(8,128)(2,1)}, bf16[512,512]{1,0:T(8,128)(2,1)S(1)}, u32[]{:S(2)}, u32[]{:S(2)}) collective-permute-start(bf16[512,512]{1,0:T(8,128)(2,1)} %bitcast.546), channel_id=1, source_target_pairs={{8,0},{9,1},{10,2},{11,3},{12,4},{13,5},{14,6},{15,7},{16,8},{17,9... | collective-permute-start | bytes 1572872 | tf_op jit(solution)/shard_map/ppermute | solution.py:44
  471.9 60.8 %collective-permute-start.26 = (bf16[512,512]{1,0:T(8,128)(2,1)}, bf16[512,512]{1,0:T(8,128)(2,1)S(1)}, u32[]{:S(2)}, u32[]{:S(2)}) collective-permute-start(bf16[512,512]{1,0:T(8,128)(2,1)} %bitcast.545), channel_id=1, source_target_pairs={{3,0},{4,1},{5,2},{6,3},{7,4},{8,5},{9,6},{10,7},{11,8},{12,9},{13... | collective-permute-start | bytes 1572872 | tf_op jit(solution)/shard_map/ppermute | solution.py:44
  473.2 59.5 %collective-permute-start.27 = (bf16[512,512]{1,0:T(8,128)(2,1)}, bf16[512,512]{1,0:T(8,128)(2,1)S(1)}, u32[]{:S(2)}, u32[]{:S(2)}) collective-permute-start(bf16[512,512]{1,0:T(8,128)(2,1)} %bitcast.544), channel_id=1, source_target_pairs={{4,0},{5,1},{6,2},{7,3},{8,4},{9,5},{10,6},{11,7},{12,8},{13,9},{1... | collective-permute-start | bytes 1572872 | tf_op jit(solution)/shard_map/ppermute | solution.py:44
  (57 other events, 927.2 us)
Sparse Core Ops, SparseCore 0:
  540.7 185.9 all-reduce.5
where the time goes:
time: 754 us; the launch traced here: 742 us
  waiting for transfers between devices  300 us (40%)
  local copies, waits for them, and re-layouts  193 us (26%)
  starting transfers between devices  121 us (16%)
  matrix products  65 us (9%)
  other arithmetic  48.3 us (6%)
  between operations  15.3 us (2%)
    psum x1, waiting for transfers between devices, local(): lax.psum(weight_terms[0].astype(jnp.bfloat16), ('dp', 'seq'))  179 us
    ppermute x32, starting transfers between devices, shifted(): return lax.ppermute(block, axis, route)  101 us
    ppermute x32, waiting for transfers between devices, shifted(): return lax.ppermute(block, axis, route)  100 us
    unnamed x142, local copies, waits for them, and re-layouts  76.9 us
    dot_general x19, matrix products, product(): return jnp.einsum(form, left, right, preferred_element_type=jnp.float32)  53.9 us
    all_to_all x1, waiting for transfers between devices, sent_to_all(): lax.all_to_all(jnp.broadcast_to(shard[None], (count, *shard.shape)), axis...  21.3 us
    another operation x9, local copies, waits for them, and re-layouts, bar_block(): jnp.stack(key_parts, 1)  20.7 us
    transpose x2, local copies, waits for them, and re-layouts, product(): return jnp.einsum(form, left, right, preferred_element_type=jnp.float32)  19.7 us
  transfers between devices with their start and end apart: 35, of which 10 were waited for; matrix products, arithmetic and copies ran while one was open for 22% of the time, Pallas kernels for 0%

commit v1 on v0

--- a/solution.py
+++ b/solution.py
@@ -1,3 +1,4 @@
+import functools
 import math
 import jax
 import jax.numpy as jnp
@@ -9,6 +10,15 @@
 bar_offsets = (0, 1, 2, 4, 8, 12, 16, 24, 32)
 group_bars = 4
 far_score = -1e30
+
+
+def name_set_over_axis(xx, axis_id, group_axis):
+    for c in (axis_id, group_axis):
+        xx = lax.psum(xx, c)
+    return xx
+
+
+put_slots = functools.partial(name_set_over_axis, axis_id="seq", group_axis="dp")
 
 
 def sent_to_all(shard, axis):
@@ -318,7 +328,7 @@
         product("te,td->ed", attended_context, grad_out),
     )
     summed = (
-        lax.psum(weight_terms[0].astype(jnp.bfloat16), ("dp", "seq")).astype(jnp.float32),
+        put_slots(weight_terms[0].astype(jnp.bfloat16)).astype(jnp.float32),
         lax.psum(weight_terms[1].astype(jnp.bfloat16), ("dp", "seq")).astype(jnp.float32),
         lax.psum(weight_terms[2].astype(jnp.bfloat16), ("dp", "seq")).astype(jnp.float32),
         lax.psum(weight_terms[3].astype(jnp.bfloat16), ("dp", "seq")).astype(jnp.float32),

time: 754 us -> 758 us (level)
  waiting for transfers between devices: 300 us -> 283 us
  starting transfers between devices: 121 us -> 133 us
  other arithmetic: 48.3 us -> 56.1 us
    ppermute x32, waiting for transfers between devices: 100 us -> 35.4 us  [shifted(): return lax.ppermute(block, axis, route)]
    psum x1 -> x3, waiting for transfers between devices: 179 us -> 226 us  [the longest x1 166 us: local(): lax.psum(weight_terms[1].astype(jnp.bfloat16), ('dp', 'seq'))]
    all_to_all x1, starting transfers between devices: 14.8 us -> 26.9 us  [sent_and_summed(): lax.all_to_all(parts, axis, split_axis=0, concat_axis=0, tiled=True)]
    unnamed x142 -> x146, local copies, waits for them, and re-layouts: 76.9 us -> 77.6 us
  transfers between devices with their start and end apart: 35 -> 37, of which waited for: 10 -> 11; matrix products, arithmetic and copies ran while one was open for 22% -> 22% of each run, Pallas kernels for 0% -> 0%
where the time goes in v1:
time: 758 us; the launch traced here: 746 us
  waiting for transfers between devices  283 us (37%)
  local copies, waits for them, and re-layouts  195 us (26%)
  starting transfers between devices  133 us (18%)
  matrix products  64.2 us (8%)
  other arithmetic  56.1 us (7%)
  between operations  15.3 us (2%)
    psum x1, waiting for transfers between devices, local(): lax.psum(weight_terms[1].astype(jnp.bfloat16), ('dp', 'seq'))  166 us
    ppermute x32, starting transfers between devices, shifted(): return lax.ppermute(block, axis, route)  102 us
    unnamed x146, local copies, waits for them, and re-layouts  77.6 us
    psum x2, waiting for transfers between devices, name_set_over_axis(): xx = lax.psum(xx, c)  60.4 us
    dot_general x19, matrix products, product(): return jnp.einsum(form, left, right, preferred_element_type=jnp.float32)  52.9 us
    ppermute x32, waiting for transfers between devices, shifted(): return lax.ppermute(block, axis, route)  35.4 us
    all_to_all x1, starting transfers between devices, sent_and_summed(): lax.all_to_all(parts, axis, split_axis=0, concat_axis=0, tiled=True)  26.9 us
    all_to_all x1, waiting for transfers between devices, sent_to_all(): lax.all_to_all(jnp.broadcast_to(shard[None], (count, *shard.shape)), axis...  21.2 us
  transfers between devices with their start and end apart: 37, of which 11 were waited for; matrix products, arithmetic and copies ran while one was open for 22% of the time, Pallas kernels for 0%

profile of v1, /device:TPU:1, one launch (start us, length us, event | category | flops | bytes accessed | tf_op | source)
XLA Modules:
  0.0 746.4 jit_solution(8840447076054307394)
XLA Ops:
  11.3 4.9 collective-permute-start.15
  20.2 5.3 collective-permute-start.10
  56.2 21.2 %all-to-all-done = bf16[32,4,1024]{2,1,0:T(4,128)(2,1)S(1)} async-done(((bf16[32,4,1024]{2,1,0:T(4,128)(2,1)}), bf16[32,4,1024]{2,1,0:T(4,128)(2,1)S(1)}, u32[]{:S(2)}, u32[]{:S(2)}) %all-to-all-start) | async-done | bytes 262176 | tf_op jit(solution)/shard_map/all_to_all | solution.py:26
  101.1 11.5 %collective-permute-done.12 = bf16[512,512]{1,0:T(8,128)(2,1)S(1)} collective-permute-done((bf16[512,512]{1,0:T(8,128)(2,1)}, bf16[512,512]{1,0:T(8,128)(2,1)S(1)}, u32[]{:S(2)}, u32[]{:S(2)}) %collective-permute-start.12) | collective-permute-done | bytes 524320 | tf_op jit(solution)/shard_map/ppermute | solution.py:54
  118.3 6.5 collective-permute-start.4
  125.6 5.1 collective-permute-start.1
  141.2 7.7 %reshape.379 = bf16[36,128,4,128]{3,2,1,0:T(4,128)(2,1)} reshape(bf16[9,512,512]{2,1,0:T(8,128)(2,1)} %rev.9) | data formatting | bytes 9437184 | tf_op jit(solution)/shard_map/reshape | solution.py:223
  159.1 25.6 %collective-permute-start.3 = (bf16[512,512]{1,0:T(8,128)(2,1)}, bf16[512,512]{1,0:T(8,128)(2,1)}, u32[]{:S(2)}, u32[]{:S(2)}) collective-permute-start(bf16[512,512]{1,0:T(8,128)(2,1)} %get-tuple-element.135), channel_id=1, source_target_pairs={{0,4},{1,5},{2,6},{3,7},{4,8},{5,9},{6,10},{7,11},{8,12},{9,13},{1... | collective-permute-start | bytes 1572872 | tf_op jit(solution)/shard_map/ppermute | solution.py:54
  216.3 5.7 copy.316
  227.6 4.8 rev.8
  232.4 7.7 %reshape.376 = bf16[36,128,4,128]{3,2,1,0:T(4,128)(2,1)} reshape(bf16[9,512,512]{2,1,0:T(8,128)(2,1)} %rev.8) | data formatting | bytes 9437184 | tf_op jit(solution)/shard_map/reshape | solution.py:224
  275.7 10.1 %fusion.16 = f32[4,128,4,128]{1,3,2,0:T(8,128)} fusion(bf16[4,1152,4,128]{3,1,2,0:T(8,128)(2,1)} %bitcast.13, f32[4,4,128,1152]{3,2,1,0:T(8,128)} %copy-done.1, f32[4,4,128]{2,1,0:T(4,128)S(1)} %copy_add_fusion.1, f32[4,4,128]{2,1,0:T(4,128)S(1)} %copy_maximum_fusion, pred[4,128,1152]{2,1,0:T(8,128)(4,1)S(1)} %broadcast_and_fusion), kind=kOutput, calls=%fused_computation.36 | convolution fusion | flops 618135552 | bytes 15810560 | tf_op jit(solution)/shard_map/while/body/eval_jaxpr/ghqk,gkhe->gqhe/dot_general | solution.py:79
  285.8 8.9 %multiply_reduce_fusion = (f32[4,4,128]{2,1,0:T(4,128)S(1)}, f32[4,4,128,1152]{3,2,1,0:T(8,128)}) fusion(f32[4,4,128]{2,1,0:T(4,128)S(1)} %copy_add_fusion.1, f32[4,4,128]{2,1,0:T(4,128)S(1)} %copy_maximum_fusion, f32[4,4,128,1152]{3,2,1,0:T(8,128)S(1)} %bitcast.496, pred[4,128,1152]{2,1,0:T(8,128)(4,1)S(1)} %broadcast_and_fusion, ...), kind=kOutput, calls=%fused_computation.1 | convolution fusion | flops 620492800 | bytes 24731648 | tf_op jit(solution)/shard_map/while/body/eval_jaxpr/gqhe,gkhe->ghqk/dot_general | solution.py:79
  294.7 5.9 convolution_bitcast_fusion
  302.1 6.6 multiply_convert_fusion
  311.3 4.9 convolution_bitcast_fusion.1
  316.3 9.8 %copy.338 = f32[4,1152,4,128]{3,1,2,0:T(8,128)} copy(f32[4,1152,4,128]{1,3,2,0:T(8,128)} %convolution_bitcast_fusion.1) | data formatting | bytes 18874368 | tf_op jit(solution)/shard_map/while/body/eval_jaxpr/ghqk,gqhe->gkhe/transpose | solution.py:79
  343.5 9.7 %copy.362 = f32[4,1152,4,128]{3,1,2,0:T(8,128)} copy(f32[4,1152,4,128]{1,3,2,0:T(8,128)} %convolution_bitcast_fusion) | data formatting | bytes 18874368 | tf_op jit(solution)/shard_map/while/body/eval_jaxpr/ghqk,gqhe->gkhe/transpose | solution.py:79
  395.4 26.9 %all-to-all-start.1 = ((bf16[32,4,8,128]{3,1,2,0:T(4,128)(2,1)}), bf16[32,4,8,128]{3,1,2,0:T(4,128)(2,1)S(1)}, u32[]{:S(2)}, u32[]{:S(2)}) async-start(bf16[32,4,8,128]{3,1,2,0:T(4,128)(2,1)} %copy.358), calls=%async_computation.1 | async-start | bytes 524288 | tf_op jit(solution)/shard_map/all_to_all | solution.py:65
  429.8 4.8 convert.15
  461.3 57.0 %all-reduce.8.cloned.1.call-done = bf16[1024,512]{0,1:T(8,128)(2,1)} async-done(((bf16[1024,512]{0,1:T(8,128)(2,1)}), bf16[1024,512]{0,1:T(8,128)(2,1)}) %all-reduce.8.cloned.1.call-update) | async-done | bytes 1048592 | tf_op jit(solution)/shard_map/psum | solution.py:17
  529.1 5.9 collective-permute-done.29
  535.0 9.9 %collective-permute-done.31 = bf16[512,512]{1,0:T(8,128)(2,1)} collective-permute-done((bf16[512,512]{1,0:T(8,128)(2,1)}, bf16[512,512]{1,0:T(8,128)(2,1)}, u32[]{:S(2)}, u32[]{:S(2)}) %collective-permute-start.31) | collective-permute-done | bytes 524320 | tf_op jit(solution)/shard_map/ppermute | solution.py:54
  566.8 165.8 %all-reduce.12.cloned.1.call-done = (bf16[1024,512]{0,1:T(8,128)(2,1)}, bf16[1024,512]{0,1:T(8,128)(2,1)}, bf16[512,1024]{1,0:T(8,128)(2,1)}) async-done(((bf16[1024,512]{0,1:T(8,128)(2,1)}, bf16[1024,512]{0,1:T(8,128)(2,1)}, bf16[512,1024]{1,0:T(8,128)(2,1)}), (bf16[1024,512]{0,1:T(8,128)(2,1)}, bf16[1024,512]{0,1:T(8,128)(2,1)}, bf16[512,1024]{1,0:T(8,128)(2,1)})) %all-reduce.12.cloned.1.call-update) | async-done | bytes 3145744 | tf_op jit(solution)/shard_map/psum | solution.py:332
  (348 shorter events, 298.9 us)
Async XLA Ops:
  11.3 121.3 %collective-permute-start.15 = (bf16[512,512]{1,0:T(8,128)(2,1)}, bf16[512,512]{1,0:T(8,128)(2,1)}, u32[]{:S(2)}, u32[]{:S(2)}) collective-permute-start(bf16[512,512]{1,0:T(8,128)(2,1)} %get-tuple-element.137), channel_id=1, source_target_pairs={{0,8},{1,9},{2,10},{3,11},{4,12},{5,13},{6,14},{7,15},{8,16},{9,17... | collective-permute-start | bytes 1572872 | tf_op jit(solution)/shard_map/ppermute | solution.py:54
  16.2 109.4 %collective-permute-start.14 = (bf16[512,512]{1,0:T(8,128)(2,1)}, bf16[512,512]{1,0:T(8,128)(2,1)}, u32[]{:S(2)}, u32[]{:S(2)}) collective-permute-start(bf16[512,512]{1,0:T(8,128)(2,1)} %get-tuple-element.137), channel_id=1, source_target_pairs={{0,7},{1,8},{2,9},{3,10},{4,11},{5,12},{6,13},{7,14},{8,15},{9,16}... | collective-permute-start | bytes 1572872 | tf_op jit(solution)/shard_map/ppermute | solution.py:54
  20.2 71.1 %collective-permute-start.10 = (bf16[512,512]{1,0:T(8,128)(2,1)}, bf16[512,512]{1,0:T(8,128)(2,1)}, u32[]{:S(2)}, u32[]{:S(2)}) collective-permute-start(bf16[512,512]{1,0:T(8,128)(2,1)} %get-tuple-element.137), channel_id=1, source_target_pairs={{0,3},{1,4},{2,5},{3,6},{4,7},{5,8},{6,9},{7,10},{8,11},{9,12},{10... | collective-permute-start | bytes 1572872 | tf_op jit(solution)/shard_map/ppermute | solution.py:54
  25.5 59.7 %collective-permute-start.9 = (bf16[512,512]{1,0:T(8,128)(2,1)}, bf16[512,512]{1,0:T(8,128)(2,1)}, u32[]{:S(2)}, u32[]{:S(2)}) collective-permute-start(bf16[512,512]{1,0:T(8,128)(2,1)} %get-tuple-element.137), channel_id=1, source_target_pairs={{0,2},{1,3},{2,4},{3,5},{4,6},{5,7},{6,8},{7,9},{8,10},{9,11},{10,... | collective-permute-start | bytes 1572872 | tf_op jit(solution)/shard_map/ppermute | solution.py:54
  28.4 52.4 %collective-permute-start.8 = (bf16[512,512]{1,0:T(8,128)(2,1)}, bf16[512,512]{1,0:T(8,128)(2,1)}, u32[]{:S(2)}, u32[]{:S(2)}) collective-permute-start(bf16[512,512]{1,0:T(8,128)(2,1)} %get-tuple-element.137), channel_id=1, source_target_pairs={{0,1},{1,2},{2,3},{3,4},{4,5},{5,6},{6,7},{7,8},{8,9},{9,10},{10,1... | collective-permute-start | bytes 1572872 | tf_op jit(solution)/shard_map/ppermute | solution.py:54
  37.0 40.4 %all-to-all-start = ((bf16[32,4,1024]{2,1,0:T(4,128)(2,1)}), bf16[32,4,1024]{2,1,0:T(4,128)(2,1)S(1)}, u32[]{:S(2)}, u32[]{:S(2)}) async-start(bf16[32,4,1024]{2,1,0:T(4,128)(2,1)} %broadcast_in_dim.191), calls=%async_computation | async-start | bytes 524288 | tf_op jit(solution)/shard_map/all_to_all | solution.py:26
  41.8 476.4 %all-reduce.8.cloned.1.call-start = ((), (), s32[]{:S(2)}) async-start(), calls=%async_computation.2 | async-start | bytes 2097152 | tf_op jit(solution)/shard_map/psum | solution.py:17
  95.4 130.3 %collective-permute-start.7 = (bf16[512,512]{1,0:T(8,128)(2,1)}, bf16[512,512]{1,0:T(8,128)(2,1)}, u32[]{:S(2)}, u32[]{:S(2)}) collective-permute-start(bf16[512,512]{1,0:T(8,128)(2,1)} %get-tuple-element.135), channel_id=1, source_target_pairs={{0,8},{1,9},{2,10},{3,11},{4,12},{5,13},{6,14},{7,15},{8,16},{9,17... | collective-permute-start | bytes 1572872 | tf_op jit(solution)/shard_map/ppermute | solution.py:54
  112.6 111.3 %collective-permute-start.6 = (bf16[512,512]{1,0:T(8,128)(2,1)}, bf16[512,512]{1,0:T(8,128)(2,1)}, u32[]{:S(2)}, u32[]{:S(2)}) collective-permute-start(bf16[512,512]{1,0:T(8,128)(2,1)} %get-tuple-element.135), channel_id=1, source_target_pairs={{0,7},{1,8},{2,9},{3,10},{4,11},{5,12},{6,13},{7,14},{8,15},{9,16}... | collective-permute-start | bytes 1572872 | tf_op jit(solution)/shard_map/ppermute | solution.py:54
  118.3 78.3 %collective-permute-start.4 = (bf16[512,512]{1,0:T(8,128)(2,1)}, bf16[512,512]{1,0:T(8,128)(2,1)}, u32[]{:S(2)}, u32[]{:S(2)}) collective-permute-start(bf16[512,512]{1,0:T(8,128)(2,1)} %get-tuple-element.135), channel_id=1, source_target_pairs={{0,5},{1,6},{2,7},{3,8},{4,9},{5,10},{6,11},{7,12},{8,13},{9,14},{... | collective-permute-start | bytes 1572872 | tf_op jit(solution)/shard_map/ppermute | solution.py:54
  154.9 35.6 %collective-permute-start.2 = (bf16[512,512]{1,0:T(8,128)(2,1)}, bf16[512,512]{1,0:T(8,128)(2,1)}, u32[]{:S(2)}, u32[]{:S(2)}) collective-permute-start(bf16[512,512]{1,0:T(8,128)(2,1)} %get-tuple-element.135), channel_id=1, source_target_pairs={{0,3},{1,4},{2,5},{3,6},{4,7},{5,8},{6,9},{7,10},{8,11},{9,12},{10... | collective-permute-start | bytes 1572872 | tf_op jit(solution)/shard_map/ppermute | solution.py:54
  371.6 68.4 %collective-permute-start.20 = (bf16[512,512]{1,0:T(8,128)(2,1)}, bf16[512,512]{1,0:T(8,128)(2,1)}, u32[]{:S(2)}, u32[]{:S(2)}) collective-permute-start(bf16[512,512]{1,0:T(8,128)(2,1)} %bitcast.490), channel_id=1, source_target_pairs={{5,0},{6,1},{7,2},{8,3},{9,4},{10,5},{11,6},{12,7},{13,8},{14,9},{... | collective-permute-start | bytes 1572872 | tf_op jit(solution)/shard_map/ppermute | solution.py:54
  372.9 68.4 %collective-permute-start.22 = (bf16[512,512]{1,0:T(8,128)(2,1)}, bf16[512,512]{1,0:T(8,128)(2,1)}, u32[]{:S(2)}, u32[]{:S(2)}) collective-permute-start(bf16[512,512]{1,0:T(8,128)(2,1)} %bitcast.488), channel_id=1, source_target_pairs={{7,0},{8,1},{9,2},{10,3},{11,4},{12,5},{13,6},{14,7},{15,8},{16,9}... | collective-permute-start | bytes 1572872 | tf_op jit(solution)/shard_map/ppermute | solution.py:54
  374.2 69.3 %collective-permute-start.21 = (bf16[512,512]{1,0:T(8,128)(2,1)}, bf16[512,512]{1,0:T(8,128)(2,1)}, u32[]{:S(2)}, u32[]{:S(2)}) collective-permute-start(bf16[512,512]{1,0:T(8,128)(2,1)} %bitcast.489), channel_id=1, source_target_pairs={{6,0},{7,1},{8,2},{9,3},{10,4},{11,5},{12,6},{13,7},{14,8},{15,9},... | collective-permute-start | bytes 1572872 | tf_op jit(solution)/shard_map/ppermute | solution.py:54
  375.5 71.5 %collective-permute-start.23 = (bf16[512,512]{1,0:T(8,128)(2,1)}, bf16[512,512]{1,0:T(8,128)(2,1)}, u32[]{:S(2)}, u32[]{:S(2)}) collective-permute-start(bf16[512,512]{1,0:T(8,128)(2,1)} %bitcast.487), channel_id=1, source_target_pairs={{8,0},{9,1},{10,2},{11,3},{12,4},{13,5},{14,6},{15,7},{16,8},{17,9... | collective-permute-start | bytes 1572872 | tf_op jit(solution)/shard_map/ppermute | solution.py:54
  391.0 57.3 %collective-permute-start.18 = (bf16[512,512]{1,0:T(8,128)(2,1)}, bf16[512,512]{1,0:T(8,128)(2,1)}, u32[]{:S(2)}, u32[]{:S(2)}) collective-permute-start(bf16[512,512]{1,0:T(8,128)(2,1)} %bitcast.492), channel_id=1, source_target_pairs={{3,0},{4,1},{5,2},{6,3},{7,4},{8,5},{9,6},{10,7},{11,8},{12,9},{13... | collective-permute-start | bytes 1572872 | tf_op jit(solution)/shard_map/ppermute | solution.py:54
  395.4 130.7 %all-to-all-start.1 = ((bf16[32,4,8,128]{3,1,2,0:T(4,128)(2,1)}), bf16[32,4,8,128]{3,1,2,0:T(4,128)(2,1)S(1)}, u32[]{:S(2)}, u32[]{:S(2)}) async-start(bf16[32,4,8,128]{3,1,2,0:T(4,128)(2,1)} %copy.358), calls=%async_computation.1 | async-start | bytes 524288 | tf_op jit(solution)/shard_map/all_to_all | solution.py:65
  422.4 141.9 %all-reduce.10.cloned.1.call-start = ((), (), s32[]{:S(2)}) async-start(), calls=%async_computation.3 | async-start | bytes 2097152 | tf_op jit(solution)/shard_map/psum | solution.py:17
  440.0 78.3 %collective-permute-start.19 = (bf16[512,512]{1,0:T(8,128)(2,1)}, bf16[512,512]{1,0:T(8,128)(2,1)}, u32[]{:S(2)}, u32[]{:S(2)}) collective-permute-start(bf16[512,512]{1,0:T(8,128)(2,1)} %bitcast.491), channel_id=1, source_target_pairs={{4,0},{5,1},{6,2},{7,3},{8,4},{9,5},{10,6},{11,7},{12,8},{13,9},{1... | collective-permute-start | bytes 1572872 | tf_op jit(solution)/shard_map/ppermute | solution.py:54
  441.3 78.3 %collective-permute-start.16 = (bf16[512,512]{1,0:T(8,128)(2,1)}, bf16[512,512]{1,0:T(8,128)(2,1)}, u32[]{:S(2)}, u32[]{:S(2)}) collective-permute-start(bf16[512,512]{1,0:T(8,128)(2,1)} %bitcast.494), channel_id=1, source_target_pairs={{1,0},{2,1},{3,2},{4,3},{5,4},{6,5},{7,6},{8,7},{9,8},{10,9},{11,1... | collective-permute-start | bytes 1572872 | tf_op jit(solution)/shard_map/ppermute | solution.py:54
  443.5 77.4 %collective-permute-start.25 = (bf16[512,512]{1,0:T(8,128)(2,1)}, bf16[512,512]{1,0:T(8,128)(2,1)}, u32[]{:S(2)}, u32[]{:S(2)}) collective-permute-start(bf16[512,512]{1,0:T(8,128)(2,1)} %bitcast.485), channel_id=1, source_target_pairs={{2,0},{3,1},{4,2},{5,3},{6,4},{7,5},{8,6},{9,7},{10,8},{11,9},{12,... | collective-permute-start | bytes 1572872 | tf_op jit(solution)/shard_map/ppermute | solution.py:54
  447.0 75.2 %collective-permute-start.28 = (bf16[512,512]{1,0:T(8,128)(2,1)}, bf16[512,512]{1,0:T(8,128)(2,1)}, u32[]{:S(2)}, u32[]{:S(2)}) collective-permute-start(bf16[512,512]{1,0:T(8,128)(2,1)} %bitcast.482), channel_id=1, source_target_pairs={{5,0},{6,1},{7,2},{8,3},{9,4},{10,5},{11,6},{12,7},{13,8},{14,9},{... | collective-permute-start | bytes 1572872 | tf_op jit(solution)/shard_map/ppermute | solution.py:54
  448.3 75.2 %collective-permute-start.30 = (bf16[512,512]{1,0:T(8,128)(2,1)}, bf16[512,512]{1,0:T(8,128)(2,1)}, u32[]{:S(2)}, u32[]{:S(2)}) collective-permute-start(bf16[512,512]{1,0:T(8,128)(2,1)} %bitcast.480), channel_id=1, source_target_pairs={{7,0},{8,1},{9,2},{10,3},{11,4},{12,5},{13,6},{14,7},{15,8},{16,9}... | collective-permute-start | bytes 1572872 | tf_op jit(solution)/shard_map/ppermute | solution.py:54
  518.3 214.4 %all-reduce.12.cloned.1.call-start = ((), (), s32[]{:S(2)}) async-start(), calls=%async_computation.4 | async-start | bytes 6291456 | tf_op jit(solution)/shard_map/psum | solution.py:332
  (61 other events, 917.3 us)
Sparse Core Ops, SparseCore 0:
  360.0 158.2 all-reduce.7
  520.7 43.5 all-reduce.9
  570.0 162.6 all-reduce.11
